TPU v7x, 32 devices: a whole 2x2x4 slice. The times are simulated.
32 devices in a mesh: gx: 8 (over z, y), gy: 4 (over x, core).
Axes of the slice: x: 2, y: 2, z: 4, core: 2. Of those that a mesh axis runs over, the one named last changes fastest.
Arguments:
- warm_start: float32 [8, 16, 128, 512], P(None, None, 'gx', 'gy'), may hold values from 0 to 39.36
- slowness: float32 [16, 128, 512], P(None, 'gx', 'gy'), may hold values from 0.02 to 0.05
- anisotropy: float32 [3, 16, 128, 512], P(None, None, 'gx', 'gy'), may hold values from 0.5 to 1.5
- observed: float32 [8, 512], P(None, ('gx', 'gy')), may hold values from 0 to 25
- station_cell: int32 [512], replicated, may hold values from 0 to 65535
- source_cell: int32 [8], replicated, may hold values from 0 to 1048575
Outputs:
- traveltime: float32 [8, 16, 128, 512], P(None, None, 'gx', 'gy')
- kernel: float32 [16, 128, 512], P(None, 'gx', 'gy')
All inputs are finite; a program needn't handle non-finite values.
Results may differ from a plain program's by a relative error of at most 0.0003.
Values sent between devices are 32-bit elements; how exact they have to be, the bound alone decides.
No kernel may reach another device: no remote copies, remote signals or barrier semaphores. Data moves between devices by JAX's collectives and lax.ppermute only.
A program may use at most 128 MiB of HBM per device.

v0:
```python
import functools
import math

import jax
import jax.numpy as jnp
from jax import lax
from jax.experimental import pallas as pl
from jax.experimental.pallas import tpu as pltpu
from jax.sharding import PartitionSpec as P

TAU = 0.05
ADJ_SCALE = 0.1
LOG2E = math.log2(math.e)
RATE = LOG2E / TAU
BIG = 10000.0 * RATE
UNROLL = 8
CHUNKS = 4
VMEM = pl.BlockSpec(memory_space=pltpu.VMEM)
FAR = pl.BlockSpec(memory_space=pl.ANY)
SMEM = pl.BlockSpec(memory_space=pltpu.SMEM)
PARAMS = pltpu.CompilerParams(vmem_limit_bytes=8 * 1024 * 1024)


def softmin(values):
    least = functools.reduce(jnp.minimum, values)
    parts = [jnp.exp2(least - v) for v in values]
    return least, parts, functools.reduce(jnp.add, parts)


def soft_pair(first, second):
    return jnp.minimum(first, second) - LOG2E * jnp.log(1.0 + jnp.exp2(-jnp.abs(first - second)))


def add_pair(least, total, passed):
    low = jnp.minimum(least, passed)
    return low - LOG2E * jnp.log(total * jnp.exp2(low - least) + jnp.exp2(low - passed))


def join_pairs(first, second):
    low = jnp.minimum(first[0], second[0])
    return low, first[1] * jnp.exp2(low - first[0]) + second[1] * jnp.exp2(low - second[0])


def value_of(pair):
    return pair[0] - LOG2E * jnp.log(pair[1])


def split_pair(first, second):
    gap = jnp.exp2(-jnp.abs(first - second))
    share = 1.0 / (1.0 + gap)
    less = gap * share
    nearer = first <= second
    return jnp.where(nearer, share, less), jnp.where(nearer, less, share)


def iota(shape, axis):
    return lax.broadcasted_iota(jnp.int32, shape, axis)


def row(ref, index, x, like):
    return jnp.broadcast_to(ref[index, pl.ds(x, 1), :], like)


def row_of(ref, x, like):
    return jnp.broadcast_to(ref[pl.ds(x, 1), :], like)


def all_steps(count, step, carry):
    for i in range(count):
        carry = step(i, carry)
    return carry


def by_steps(count, step, carry):
    def group(i, carry):
        for j in range(UNROLL):
            carry = step(i * UNROLL + j, carry)
        return carry

    return lax.fori_loop(0, count // UNROLL, group, carry)


def packed(left, right):
    return jnp.where(iota(left.shape, 0) < 5, left, pltpu.roll(right, 2, 0))


def merged(left, right):
    return jnp.where(iota(left.shape, 0) < 4, left, right)


def shifted_down(tile, by):
    return pltpu.roll(tile, tile.shape[0] - by, 0)


def exact_parts(value):
    high = value.astype(jnp.bfloat16).astype(jnp.float32)
    middle = (value - high).astype(jnp.bfloat16).astype(jnp.float32)
    low = value - high - middle
    return [p.astype(jnp.bfloat16) for p in (high, middle, low)]


def pack_kernel(
    place, source_far, warm_far, observed_far, slowness_far, anisotropy_far, start, costs, near, edge, to_right, to_left, records,
    source, warm, observed, slowness, anisotropy, arrived,
):
    pairs = [(slowness_far, slowness), (anisotropy_far, anisotropy), (observed_far, observed)]
    share = start.shape[1] // CHUNKS
    span = share * start.shape[0]
    pairs += [(warm_far.at[:, pl.ds(i * span, span)], warm.at[i]) for i in range(CHUNKS)]
    pairs += [(source_far, source)]
    copies = [pltpu.make_async_copy(a, b, arrived.at[i]) for i, (a, b) in enumerate(pairs)]
    for copy in copies:
        copy.start()
    width_x, depth, quakes, width_y = start.shape
    tile = (quakes, width_y)
    quake = iota(tile, 0)
    lane = iota(tile, 1)
    span_y = place[2]
    plane = place[3]
    rows = width_x * 8
    wide = (width_x, width_y)
    group = iota(wide, 1) >> 3
    copies[0].wait()
    copies[1].wait()
    native = []
    for k in range(3):
        columns = jnp.zeros(wide, jnp.float32)
        for z in range(depth):
            cost = slowness[z] * anisotropy[k * depth + z] * RATE
            costs[k * depth + z] = cost
            columns = jnp.where(group == z, pltpu.roll(cost, 8 * z + 4, 1), columns)
        edge[rows : rows + width_x, :] = columns
        rows += width_x
        native.append(columns)
        for z in range(near.shape[0] // 3):
            near[k * (near.shape[0] // 3) + z] = anisotropy[k * depth + z]
    early = (iota(wide, 1) & 7) < 4
    at = slice(4 * width_x, 5 * width_x)
    to_right[at, :] = jnp.where(early, native[0], pltpu.roll(native[1], 4, 1))
    to_left[at, :] = jnp.where(early, pltpu.roll(native[1], width_y - 4, 1), native[0])
    at = slice(5 * width_x, 6 * width_x)
    to_right[at, :] = native[2]
    to_left[at, :] = native[2]
    copies[-1].wait()
    cell = jnp.zeros(tile, jnp.int32)
    for e in range(quakes):
        cell = jnp.where(quake == e, source[e], cell)
    cell = cell - (lane + place[0] * span_y + place[1])
    edges = []
    for i in range(CHUNKS):
        copies[3 + i].wait()
        here = warm.at[i].reshape(quakes * share * width_x, width_y)

        chunk = [jnp.zeros(tile, jnp.float32)] * share
        for x in range(width_x):
            mine = (lane >> 3) == x
            for k in range(share):
                value = here[pl.ds(k * width_x + x, quakes, stride=share * width_x), :] * RATE
                value = jnp.where(cell == (i * share + k) * plane + x * span_y, 0.0, value)
                start[x, i * share + k] = value
                chunk[k] = jnp.where(mine, pltpu.roll(value, (8 * x + 4) % width_y, 1), chunk[k])
        edges += chunk
    columns = jnp.transpose(jnp.concatenate(edges, 0))
    edge[: width_x * 8, :] = columns
    low = quake < 4
    for x in range(0, width_x, 2):
        one, two = columns[8 * x : 8 * x + 8], columns[8 * x + 8 : 8 * x + 16]
        to_right[4 * x : 4 * x + 8, :] = jnp.where(low, one, pltpu.roll(two, 4, 0))
        to_left[4 * x : 4 * x + 8, :] = jnp.where(low, pltpu.roll(one, 4, 0), two)
    copies[2].wait()
    records[...] = jnp.zeros(tile, jnp.float32)
    records[:, : observed.shape[1]] = observed[...]
    for message in (to_right, to_left):
        message[6 * width_x :, :] = records[...]


def halo_columns(left, right):
    rows = []
    for l, r in zip(left, right):
        rows.append(jnp.where(iota(l.shape, 0) == 4, r, pltpu.roll(l, 2, 0)))
    return jnp.transpose(jnp.concatenate(rows, 0))


def cost_columns(message, width_x, turn):
    pair = message[4 * width_x : 5 * width_x, :]
    return [pair, pltpu.roll(pair, turn, 1), message[5 * width_x : 6 * width_x, :]]


def strip_costs(own, from_left, from_right, out, width_x, depth):
    tile = own.shape[1]
    base = width_x * 8
    lane = iota((8, tile), 1)
    low = (lane & 7) < 4
    mine = (lane & 7) == iota((8, tile), 0)
    spread = ((iota((tile, tile), 0) >> 3) == (iota((tile, tile), 1) >> 3)).astype(jnp.float32)
    spread = spread.astype(jnp.bfloat16)
    for side in range(2):
        for k in range(3):
            rows = []
            for x in range(width_x):
                at = slice(base + k * width_x + x, base + k * width_x + x + 1)
                here = jnp.broadcast_to(own[at, :], lane.shape)
                there = jnp.broadcast_to((from_right if side else from_left)[k][x : x + 1], lane.shape)
                value = jnp.where(low, here, there) if side else jnp.where(low, there, here)
                rows.append(jnp.where(mine, value, 0.0))
            whole = jnp.concatenate(rows, 0)
            total = 0.0
            for part in reversed(exact_parts(whole)):
                total = total + lax.dot_general(
                    part, spread, (((1,), (0,)), ((), ())), preferred_element_type=jnp.float32
                )
            out[3 * side + k] = total.reshape(width_x, 8, tile)


def running_sum(value):
    rows = iota(value.shape, 0)
    by = 1
    while by < value.shape[0]:
        value = value + jnp.where(rows >= by, pltpu.roll(value, by, 0), 0.0)
        by *= 2
    return value


def log_sum(exponents):
    return -LOG2E * jnp.log(functools.reduce(jnp.add, [jnp.exp2(-e) for e in exponents]))


def passages(costs, from_left, from_right, depth):
    width_x, width_y = costs.shape[1:]
    lane = iota((width_x, width_y), 1)
    beside = jnp.where((lane & 7) == 4, running_sum(from_right), pltpu.roll(running_sum(from_left), 2, 1))
    sums = [running_sum(costs[z]) for z in range(depth)]
    sub = iota((8, width_y), 0)
    tiles = []
    for z in range(depth):
        back = sums[z] - costs[z]
        edge = pltpu.roll(beside, width_y - 5 - 8 * z, 1)
        below = jnp.where(lane == 0, edge, pltpu.roll(sums[z], 1, 1))
        above = jnp.where(lane == width_y - 1, edge, pltpu.roll(sums[z], width_y - 1, 1))
        step_y = back + costs[depth + z]
        step_z = back + costs[2 * depth + z]
        paths = [sums[z] + back, below + step_y, above + step_y]
        paths.append(sums[z - 1] + step_z if z > 0 else None)
        paths.append(sums[z + 1] + step_z if z < depth - 1 else None)
        tile = jnp.broadcast_to(sums[z][width_x - 1 :, :], sub.shape)
        for j, path in enumerate(paths):
            if path is None:
                tile = jnp.where(sub == j + 1, BIG, tile)
            else:
                total = jnp.sum(jnp.exp2(-path), axis=0, keepdims=True)
                tile = jnp.where(sub == j + 1, -LOG2E * jnp.log(total), tile)
        tiles.append(tile)
    return tiles


def strip_passages(edge_costs, width_x):
    shape = edge_costs.shape[2:]
    lane = iota(shape, 1)
    sums = jnp.zeros(shape, jnp.float32)
    totals = [jnp.zeros(shape, jnp.float32)] * 5
    for x in range(width_x):
        cost, step_y, step_z = [packed(edge_costs[k, x], edge_costs[3 + k, x]) for k in range(3)]
        back = sums
        sums = sums + cost
        step_y, step_z = step_y + back, step_z + back
        paths = [sums + back, pltpu.roll(sums, 1, 0) + step_y, shifted_down(sums, 1) + step_y]
        paths.append(jnp.where(lane < 8, BIG, pltpu.roll(sums, 8, 1) + step_z))
        paths.append(jnp.where(lane >= shape[1] - 8, BIG, pltpu.roll(sums, shape[1] - 8, 1) + step_z))
        totals = [t + jnp.exp2(-p) for t, p in zip(totals, paths)]
    return sums, [-LOG2E * jnp.log(jnp.maximum(t, 1e-37)) for t in totals]


def shared_rows(total, paths):
    place = iota(total.shape, 1) & 7
    first, second = total, total
    for q in range(6):
        value = pltpu.roll(total, (4 - q) % 8, 0)
        first = jnp.where(place == q, value, first)
    for q, (path, at) in enumerate([(p, r) for p in paths for r in (3, 6)]):
        if q < 2:
            first = jnp.where(place == 6 + q, pltpu.roll(path, (6 - at) % 8, 0), first)
        else:
            second = jnp.where(place == q - 2, pltpu.roll(path, (7 - at) % 8, 0), second)
    return jnp.where(iota(total.shape, 0) == 6, first, second)


def spread_rows(tiles):
    shape = tiles[0].shape
    wide = shape[1]
    sub = iota(shape, 0)
    mine = (iota(shape, 1) & 7) == sub
    spread = ((iota((wide, wide), 0) >> 3) == (iota((wide, wide), 1) >> 3)).astype(jnp.float32)
    spread = spread.astype(jnp.bfloat16)
    rows = [jnp.where(mine, jnp.broadcast_to(t[r : r + 1], shape), 0.0) for t in tiles for r in (6, 7)]
    whole = jnp.concatenate(rows, 0)
    value = 0.0
    for part in reversed(exact_parts(whole)):
        value = value + lax.dot_general(part, spread, (((1,), (0,)), ((), ())), preferred_element_type=jnp.float32)
    out = []
    for i in range(len(tiles)):
        first, second = value[16 * i : 16 * i + 8], value[16 * i + 8 : 16 * i + 16]
        paths = [jnp.where(sub == 3, pltpu.roll(first, 5, 0), pltpu.roll(first, 7, 0))]
        for q in range(4):
            at_three = pltpu.roll(second, (3 - 2 * q) % 8, 0)
            at_six = pltpu.roll(second, (6 - 2 * q - 1) % 8, 0)
            paths.append(jnp.where(sub == 3, at_three, at_six))
        out.append((pltpu.roll(first, 2, 0), paths))
    return out


def sweep_step(x, near, levels, strip, costs, edge_costs, halo, state, strip_state, keep, keep_strip):
    depth = costs.shape[0] // 3
    tile = levels[0].shape
    width_y = tile[1]
    lane = iota(tile, 1)
    out = []
    for z in range(len(state)):
        u = levels[z]
        cost_y = row(costs, depth + z, x, tile)
        cost_z = row(costs, 2 * depth + z, x, tile)
        edge = pltpu.roll(halo[z], width_y - 5 - 8 * x, 1)
        values = [u]
        values.append(jnp.where(lane == 0, edge, pltpu.roll(u, 1, 1)) + cost_y)
        values.append(jnp.where(lane == width_y - 1, edge, pltpu.roll(u, width_y - 1, 1)) + cost_y)
        if z > 0:
            values.append(levels[z - 1] + cost_z)
        if z < depth - 1:
            values.append(levels[z + 1] + cost_z)
        least, parts, total = softmin(values)
        passed = state[z] + row(costs, z, x, tile)
        if z < near:
            scale = 1.0 / total
            keep(x, z, value_of((least, total)), [p * scale for p in parts], passed)
        out.append(add_pair(least, total, passed))
    strips, relaxed, weights, passes = [], [], [], []
    for side in range(2 if strip is not None else 0):
        u = strip[x, side]
        cost_y = edge_costs[3 * side + 1, x]
        cost_z = edge_costs[3 * side + 2, x]
        values = [u, pltpu.roll(u, 1, 0) + cost_y, pltpu.roll(u, 7, 0) + cost_y]
        values.append(jnp.where(lane < 8, BIG, pltpu.roll(u, 8, 1)) + cost_z)
        values.append(jnp.where(lane >= width_y - 8, BIG, pltpu.roll(u, width_y - 8, 1)) + cost_z)
        least, parts, total = softmin(values)
        passes.append(strip_state[side] + edge_costs[3 * side, x])
        strips.append(add_pair(least, total, passes[side]))
        if keep_strip is not None:
            relaxed.append(value_of((least, total)))
            weights.append(parts[2 - side] / total)
    if keep_strip is not None:
        keep_strip(x, merged(*relaxed), merged(*weights), merged(*passes), merged(*strips))
    return out, strips


def outside_strips(place, shape):
    sub = iota(shape, 0)
    return [(place[4] == 1) & (sub < 4), (place[5] == 1) & (sub >= 4)]


def first_sweep_kernel(
    rows_of, count_y, per, place, field, own, mine, from_left, from_right, costs, anisotropy, *rest
):
    others = rest[: count_y - 3]
    local, local_strip, edge_costs, levels, sides, message, halo, strip = rest[count_y - 3 :]
    width_x, depth, quakes, width_y = field.shape
    tile = (quakes, width_y)
    sub = iota(tile, 0)
    low = sub < 4
    near = levels.shape[1]
    last = 6 * width_x
    far = [mine[...], from_left[last:, :]] + [o[...] for o in others] + [from_right[last:, :]]
    records = jnp.zeros(tile, jnp.float32)
    for by, piece in enumerate(far):
        owner = lax.rem(place[8] + count_y - by, count_y)
        records = records + pltpu.roll(piece, owner * rows_of, 1)
    left, right = [], []
    for x in range(width_x):
        at = slice(8 * x, 8 * x + 8)
        two = slice(8 * (x // 2), 8 * (x // 2) + 8)
        before, after = from_left[two, :], from_right[two, :]
        if x % 2:
            before = pltpu.roll(before, 4, 0)
        else:
            after = pltpu.roll(after, 4, 0)
        before = jnp.where(place[4] == 1, BIG, before)
        after = jnp.where(place[5] == 1, BIG, after)
        left.append(jnp.where(low, before, own[at, :]))
        right.append(jnp.where(low, own[at, :], after))
        strip[x, 0] = left[x]
        strip[x, 1] = right[x]
    halo[...] = halo_columns(left, right).reshape(halo.shape)
    left_costs = cost_columns(from_left, width_x, width_y - 4)
    right_costs = cost_columns(from_right, width_x, 4)
    strip_costs(own, left_costs, right_costs, edge_costs, width_x, depth)
    outside = outside_strips(place, tile)

    def keep(x, z, level, w, passed):
        levels[x, z] = level
        vertical = w[3] if z == 0 else w[3] + w[4]
        sideways = row(anisotropy, near + z, x, tile) * (w[1] + w[2])
        sides[x, z] = sideways + row(anisotropy, 2 * near + z, x, tile) * vertical

    def step(x, carry):
        state, strips = sweep_step(x, near, [field[x, z] for z in range(depth)], strip, costs, edge_costs, halo, *carry, keep, None)
        for z in range(depth):
            local[x, z] = state[z]
        for side in range(2):
            local_strip[x, side] = jnp.where(outside[side], BIG, strips[side])
        return state, strips

    blank = jnp.full(tile, BIG, jnp.float32)
    state, strips = all_steps(width_x, step, ([blank] * depth, [blank] * 2))
    reach_strip = packed(*[jnp.where(o, BIG, s) for o, s in zip(outside, strips)])

    edges = [[local_strip[x, side] for x in range(width_x)] for side in range(2)]
    halo[...] = halo_columns(*edges).reshape(halo.shape)

    def again(lap, carry):
        x = width_x - 1 - lap
        values = [local[x, z] for z in range(depth)]
        return sweep_step(x, 0, values, local_strip, costs, edge_costs, halo, *carry, None, None)

    back, back_strips = all_steps(width_x, again, ([blank] * depth, [blank] * 2))
    tiles = passages(costs, left_costs[0], right_costs[0], depth)
    strip_total, strip_paths = strip_passages(edge_costs, width_x)

    back_strip = packed(*back_strips)
    reach_strip = jnp.where(sub == 0, shifted_down(back_strip, 3), reach_strip)
    reach_strip = jnp.where(sub == 1, shifted_down(back_strip, 5), reach_strip)
    shared = shared_rows(strip_total, strip_paths)
    count = message.shape[0]
    for p in range(count):
        first = min(p * per, depth - per)
        for k in range(per + 2):
            z = first + k - 1
            message[p, k] = state[z] if 0 <= z < depth else blank
        for k in range(per):
            message[p, per + 2 + k] = back[first + k]
            value = tiles[first + k]
            if k == 0 and first > 0:
                value = jnp.where(sub == 6, jnp.broadcast_to(tiles[first - 1][:1], tile), value)
            if k == 0 and first + per < depth:
                value = jnp.where(sub == 7, jnp.broadcast_to(tiles[first + per][:1], tile), value)
            if per > 1 and k == 1:
                value = jnp.where(sub < 6, value, shared)
            message[p, 2 * per + 2 + k] = value
        message[p, 3 * per + 2] = reach_strip
        message[p, 3 * per + 3] = records
        if per == 1:
            message[p, 3 * per + 4] = shared
        surface = [state[0], state[1], back[0], jnp.where(sub < 6, tiles[0], jnp.broadcast_to(tiles[1][:1], tile))]
        for i, value in enumerate(surface):
            message[p, message.shape[1] - 4 + i] = value


def owner_carries(
    per, depth, place, received, entering, entering_strips, surface_edges, halo,
):
    count = received.shape[0]
    tile = entering.shape[2:]
    lane = iota(tile, 1)
    width_y = tile[1]
    me = place[6]
    blank = jnp.full(tile, BIG, jnp.float32)
    unit = jnp.ones(tile, jnp.float32)
    side = 3 * per + 2

    def rows(device, k, j):
        return jnp.broadcast_to(received[device, 2 * per + 2 + k, j : j + 1, :], tile)

    def total(device, k):
        if k < 0:
            return rows(device, 0, 6)
        return rows(device, k, 0) if k < per else rows(device, 0, 7)

    def further(pair, cost):
        return pair[0] + cost, pair[1]

    shared = [received[d, 2 * per + 3] if per > 1 else received[d, 3 * per + 4] for d in range(count)]
    shared = spread_rows(shared)
    state = [(blank, unit)] * (per + 2)
    strip = (blank, unit)
    first, first_strip = [], []
    for device in range(count):
        first.append([value_of(pair) for pair in state])
        first_strip.append(value_of(strip))
        state = [
            join_pairs((received[device, k], unit), further(state[k], total(device, k - 1))) for k in range(per + 2)
        ]
        strip = join_pairs((received[device, side], unit), further(strip, shared[device][0]))
    own = blank
    for device in range(count):
        own = jnp.where(device == me, first_strip[device], own)
        for k in range(per):
            entering[device, k] = first[device][k + 1]
    entering_strips[0] = own
    group = width_y // 8
    for at in range(0, count, group):
        some = first_strip[at : at + group]
        some = some + [blank] * (group - len(some))
        turned = halo_columns(some, [shifted_down(s, 2) for s in some])
        halo[at // group] = turned.reshape(halo.shape[1:])
        surface_edges[at // group] = turned[: tile[0]]
    low = jnp.minimum(me * per, depth - per)
    edges = [[halo[i, low + k] for k in range(per)] for i in range(halo.shape[0])]
    state = [(blank, unit)] * per
    strip = (blank, unit)
    for device in reversed(range(count)):
        for k in range(per):
            entering[device, per + k] = value_of(state[k])
            u = first[device][k + 1]
            turn = (width_y - 5 - 8 * (device % group)) % width_y
            edge = pltpu.roll(edges[device // group][k], turn, 1)
            values = [received[device, per + 2 + k], u + rows(device, k, 1)]
            values.append(jnp.where(lane == 0, edge, pltpu.roll(u, 1, 1)) + rows(device, k, 2))
            values.append(jnp.where(lane == width_y - 1, edge, pltpu.roll(u, width_y - 1, 1)) + rows(device, k, 3))
            values.append(first[device][k] + rows(device, k, 4))
            values.append(first[device][k + 2] + rows(device, k, 5))
            least, _, amount = softmin(values)
            state[k] = join_pairs((least, amount), further(state[k], total(device, k)))
        u = first_strip[device]
        back = received[device, side]
        back = jnp.where(iota(tile, 0) == 3, pltpu.roll(back, 3, 0), pltpu.roll(back, 5, 0))
        paths = shared[device][1]
        values = [back, u + paths[0], pltpu.roll(u, 1, 0) + paths[1], shifted_down(u, 1) + paths[2]]
        values.append(jnp.where(lane < 8, BIG, pltpu.roll(u, 8, 1)) + paths[3])
        values.append(jnp.where(lane >= width_y - 8, BIG, pltpu.roll(u, width_y - 8, 1)) + paths[4])
        least, _, amount = softmin(values)
        passed = join_pairs((least, amount), further(strip, shared[device][0]))
        strip = [jnp.where(device > me, new, old) for new, old in zip(passed, strip)]
    entering_strips[1] = value_of(strip)


def middle_kernel(
    per, rows_of, place, cell, received, first, first_strip, costs, edge_costs, anisotropy, levels_one, sides,
    halo, shares, slopes, keeps, misfits, edges_own, edges_factor, slopes_one, gains, message,
    entering_strips, surface_edges, block_halo, strip, shares_strip, slopes_strip, keeps_strip, misfits_strip, sums, counts, sums_strip, counts_strip,
):
    owner_carries(per, first.shape[1], place, received, message, entering_strips, surface_edges, block_halo)
    width_x, near, quakes, width_y = levels_one.shape
    tile = (quakes, width_y)
    lane = iota(tile, 1)
    count = received.shape[0]
    base = received.shape[1] - 4
    me = place[6]
    add_records(rows_of, 3 * per + 3, place, cell, received, sums, counts, sums_strip, counts_strip)
    blank = jnp.full(tile, BIG, jnp.float32)
    unit = jnp.ones(tile, jnp.float32)

    def rows(device, j):
        return jnp.broadcast_to(received[device, base + 3, j : j + 1, :], tile)

    state = [(blank, unit)] * near
    into = []
    for device in range(count):
        into.append([value_of(pair) for pair in state])
        state = [
            join_pairs((received[device, base + z], unit), (state[z][0] + rows(device, 6 * z), state[z][1]))
            for z in range(near)
        ]
    carried = [blank] * near
    for device in range(count):
        carried = [jnp.where(device == me, new, old) for new, old in zip(into[device], carried)]
    back = (blank, unit)
    group = width_y // 8
    for device in reversed(range(count)):
        u, deeper = into[device]
        edge = pltpu.roll(surface_edges[device // group], (width_y - 5 - 8 * (device % group)) % width_y, 1)
        values = [received[device, base + 2], u + rows(device, 1), deeper + rows(device, 5)]
        values.append(jnp.where(lane == 0, edge, pltpu.roll(u, 1, 1)) + rows(device, 2))
        values.append(jnp.where(lane == width_y - 1, edge, pltpu.roll(u, width_y - 1, 1)) + rows(device, 3))
        least, _, amount = softmin(values)
        passed = join_pairs((least, amount), (back[0] + rows(device, 0), back[1]))
        back = [jnp.where(device > me, new, old) for new, old in zip(passed, back)]
    back = value_of(back)

    outside = outside_strips(place, tile)
    strips_in = [[s, shifted_down(s, 2)] for s in (entering_strips[0], entering_strips[1])]
    running = [jnp.zeros(tile, jnp.float32)] * (near + 2)
    prior = carried
    close = []
    for x in range(width_x):
        values = []
        for z in range(near):
            cost = row(costs, z, x, tile)
            running[z] = running[z] + cost
            values.append(soft_pair(first[x, z], carried[z] + running[z]))
            keep, slope = split_pair(levels_one[x, z], prior[z] + cost)
            slopes_one[x, z] = slope
            gains[x, z] = slope * row(anisotropy, z, x, tile) + keep * sides[x, z]
        prior = values
        close.append(values)
        for side in range(2):
            running[near + side] = running[near + side] + edge_costs[3 * side, x]
            value = soft_pair(first_strip[x, side], strips_in[0][side] + running[near + side])
            strip[x, side] = jnp.where(outside[side], BIG, value)
    edges = [[strip[x, side] for x in range(width_x)] for side in range(2)]
    halo[...] = halo_columns(*edges).reshape(halo.shape)

    def keep(x, z, level, w, passed):
        for i in range(4):
            shares[i, x] = w[i]
        keeps[x], slopes[x] = split_pair(level, passed)

    def keep_strip(x, level, w, passed, value):
        shares_strip[x] = w
        keeps_strip[x], slopes_strip[x] = split_pair(level, passed)
        tally = pltpu.roll(counts_strip[...], (width_y - 8 * x) % width_y, 1)
        total = pltpu.roll(sums_strip[...], (width_y - 8 * x) % width_y, 1)
        misfits_strip[x] = ADJ_SCALE * (tally * (value * (1.0 / RATE)) - total)

    def step(lap, carry):
        x = width_x - 1 - lap
        state, strips = sweep_step(x, 1, close[x], strip, costs, edge_costs, halo, *carry, keep, keep_strip)
        misfits[x] = ADJ_SCALE * (row_of(counts, x, tile) * (state[0] * (1.0 / RATE)) - sums[x])
        return state, strips

    all_steps(width_x, step, ([back], strips_in[1]))
    zero = jnp.zeros(tile, jnp.float32)
    own, factor, strip_own, strip_factor = zero, unit, zero, unit
    owns, factors = [], []
    sent = [zero, zero]
    for x in range(width_x):
        own = misfits[x] + own
        owns.append(keeps[x] * own)
        factors.append(keeps[x] * factor)
        own, factor = slopes[x] * own, slopes[x] * factor
        strip_own = misfits_strip[x] + strip_own
        through = keeps_strip[x] * shares_strip[x]
        for i, value in enumerate((strip_own, strip_factor)):
            value = pltpu.roll(through * value, 8 * x, 1) if x else through * value
            sent[i] = jnp.where((lane >> 3) == x, value, sent[i])
        strip_own, strip_factor = slopes_strip[x] * strip_own, slopes_strip[x] * strip_factor
    edges_own[...] = end_columns(sent[0]).reshape(edges_own.shape)
    edges_factor[...] = end_columns(sent[1]).reshape(edges_factor.shape)
    chain = [unit] * near
    blocks = [zero] * near
    links = [zero] * 4
    for x in range(width_x):
        entry = entries_of(owns[x], shares, x, edges_own[x])
        for z in range(near):
            chain[z] = chain[z] * slopes_one[x, z]
            blocks[z] = blocks[z] + chain[z] * entry[z]
        for i, path in enumerate(ways_of(factors[x], shares, x, edges_factor[x])):
            links[i] = links[i] + chain[i // 3] * path
    both = jnp.where(iota(tile, 0) < 5, strip_own, pltpu.roll(strip_factor, 2, 0))
    tiles = [own, factor, both] + blocks + chain + links
    for p in range(message.shape[0]):
        for i, value in enumerate(tiles):
            message[p, 2 * per + i] = value


def end_columns(rows):
    wide = rows.shape[1]
    first, last = shifted_down(rows, 3), pltpu.roll(rows, 3, 0)
    return jnp.transpose(jnp.concatenate([first] * (wide // 16) + [last] * (wide // 16), 0))


def ways_of(passed, shares, x, edge):
    lane = iota(passed.shape, 1)
    last = passed.shape[1] - 1
    above = jnp.where(lane == last, edge, pltpu.roll(passed * shares[1, x], last, 1))
    below = jnp.where(lane == 0, edge, pltpu.roll(passed * shares[2, x], 1, 1))
    return passed * shares[0, x], above, below, passed * shares[3, x]


def entries_of(passed, shares, x, edge):
    own, above, below, deeper = ways_of(passed, shares, x, edge)
    return own + above + below, deeper


def add_records(rows_of, tile_of, place, cell, received, sums, counts, sums_strip, counts_strip):
    width_x, quakes, width_y = sums.shape
    last = tile_of
    span_y = place[2]
    lane = iota((quakes, width_y), 1)
    column = iota((width_y, width_y), 0)
    strip_column = iota((8, width_y), 0)
    strip_column = jnp.where(strip_column == 3, -1, jnp.where(strip_column == 4, width_y, -2))
    share = width_y // rows_of
    dims = (((1,), (1,)), ((), ()))
    one_x = iota((width_x, width_y), 0)
    parts = [[], [], []]
    at, at_rows, at_strip = [], [], []
    for chunk in range(cell.shape[0]):
        records = jnp.zeros((quakes, width_y), jnp.float32)
        for part in range(share):
            piece = received[chunk * share + part, last]
            moved = pltpu.roll(piece, part * rows_of, 1) if part else piece
            records = jnp.where(lane // rows_of == part, moved, records)
        cells = cell[chunk : chunk + 1, :]
        station_x = lax.shift_right_logical(cells, place[7]) - place[0]
        station_y = (cells & (span_y - 1)) - place[1]
        at_x = (one_x == jnp.broadcast_to(station_x, one_x.shape)).astype(jnp.float32)
        pieces = [p.astype(jnp.float32) for p in exact_parts(records)]
        for out, piece in zip(parts, pieces):
            spread = [piece * jnp.broadcast_to(at_x[x : x + 1], piece.shape) for x in range(width_x)]
            out.append(jnp.concatenate(spread, 0).astype(jnp.bfloat16))
        at_rows.append(at_x.astype(jnp.bfloat16))
        hit = column == jnp.broadcast_to(station_y, column.shape)
        at.append(hit.astype(jnp.float32).astype(jnp.bfloat16))
        hit = strip_column == jnp.broadcast_to(station_y, strip_column.shape)
        at_strip.append(hit.astype(jnp.float32).astype(jnp.bfloat16))
    at = jnp.concatenate(at, 1)
    at_rows = jnp.concatenate(at_rows, 1)
    at_strip = jnp.concatenate(at_strip, 1)
    parts = [jnp.concatenate(p, 1) for p in parts]

    def product(a, b):
        return lax.dot_general(a, b, dims, preferred_element_type=jnp.float32)

    main = [product(p, at) for p in parts]
    sums[...] = (main[0] + main[1] + main[2]).reshape(sums.shape)
    counts[...] = product(at_rows, at)
    sums_strip[...] = product(at_strip, parts[0]) + product(at_strip, parts[1]) + product(at_strip, parts[2])
    spread = ((iota((width_x, width_y), 1) >> 3) == one_x).astype(jnp.float32).astype(jnp.bfloat16)
    tally = 0.0
    for part in reversed(exact_parts(product(at_strip, at_rows))):
        tally += lax.dot_general(part, spread, (((1,), (0,)), ((), ())), preferred_element_type=jnp.float32)
    counts_strip[...] = tally


def traveltimes(per, first, entering, costs, halo, times, field):
    width_x, depth, quakes, width_y = first.shape
    tile = (quakes, width_y)
    carried = [[entering[z // per, k * per + z % per] for z in range(depth)] for k in range(2)]

    def finish(x, running):
        sums = [running[z] + row(costs, z, x, tile) for z in range(depth)]
        for z in range(depth):
            field[x, z] = soft_pair(first[x, z], carried[0][z] + sums[z])
        return sums

    all_steps(width_x, finish, [jnp.zeros(tile, jnp.float32)] * depth)

    def step(lap, state):
        x = width_x - 1 - lap
        values = [field[x, z] for z in range(depth)]
        state, _ = sweep_step(x, 0, values, None, costs, None, halo, state, None, None, None)
        for z in range(depth):
            times[pl.ds(z * width_x + x, quakes, stride=depth * width_x), :] = state[z] * (1.0 / RATE)
        return state

    all_steps(width_x, step, carried[1])


def last_kernel(
    per, place, received, first, costs, halo, shares, slopes, keeps, misfits, edges_own, edges_factor, slopes_one,
    gains, anisotropy, times, kernel, field, value, copied, entries, top, sent,
):
    traveltimes(per, first, received, costs, halo, value, field)
    copy = pltpu.make_async_copy(value, times, copied)
    copy.start()
    adjoint(
        2 * per, place, received, shares, slopes, keeps, misfits, edges_own, edges_factor, slopes_one, gains, anisotropy,
        kernel, entries, top, sent,
    )
    copy.wait()


def adjoint(
    base, place, received, shares, slopes, keeps, misfits, edges_own, edges_factor, slopes_one, gains, anisotropy, kernel,
    entries, top, sent,
):
    width_x, quakes, width_y = slopes.shape
    tile = (quakes, width_y)
    near = slopes_one.shape[1]
    count = received.shape[0]
    lane = iota(tile, 1)
    last = width_y - 1
    me = place[6]
    zero = jnp.zeros(tile, jnp.float32)
    group = width_y // 8
    state, strip, mine, mine_strip = zero, zero, zero, zero
    carries = []
    for device in range(count):
        carries.append(state)
        mine = jnp.where(device == me, state, mine)
        at = device % group
        moved = pltpu.roll(strip, 8 * at, 1) if at else strip
        sent[device // group] = moved if at == 0 else jnp.where((lane >> 3) == at, moved, sent[device // group])
        both = received[device, base + 2]
        state = received[device, base] + received[device, base + 1] * state
        strip = both + shifted_down(both, 2) * strip
    ends = [end_columns(sent[i]) for i in range(sent.shape[0])]
    state = [zero] * near
    mine_edge = zero
    for device in reversed(range(count)):
        at = 8 * (device % group)
        edge = ends[device // group][at : at + 8]
        mine_edge = jnp.where(device == me, edge, mine_edge)
        carry = carries[device]
        block = [received[device, base + 3 + z] for z in range(near)]
        above = jnp.where(lane == last, edge, pltpu.roll(carry, last, 1))
        below = jnp.where(lane == 0, edge, pltpu.roll(carry, 1, 1))
        link = [received[device, base + 3 + 2 * near + i] for i in range(4)]
        block[0] = block[0] + link[0] * carry + link[1] * above + link[2] * below
        block[1] = block[1] + link[3] * carry
        for z in range(near):
            passed = block[z] + received[device, base + 3 + near + z] * state[z]
            state[z] = jnp.where(device > me, passed, state[z])
    carry = mine
    for x in range(width_x):
        total = misfits[x] + carry
        carry = slopes[x] * total
        passed = keeps[x] * total
        sideways = row(anisotropy, near, x, tile) * (shares[1, x] + shares[2, x])
        sideways = sideways + row(anisotropy, 2 * near, x, tile) * shares[3, x]
        terms = carry * row(anisotropy, 0, x, tile) + passed * sideways
        top[x : x + 1, :] = jnp.sum(terms, axis=0, keepdims=True)
        entry = entries_of(passed, shares, x, edges_own[x] + edges_factor[x] * mine_edge)
        for z in range(near):
            entries[x, z] = entry[z]
    for x in reversed(range(width_x)):
        for z in range(near):
            total = entries[x, z] + state[z]
            state[z] = slopes_one[x, z] * total
            value = jnp.sum(total * gains[x, z], axis=0, keepdims=True)
            if z == 0:
                value = value + top[x : x + 1, :]
            kernel[z, x : x + 1, :] = value
    for z in range(near, kernel.shape[0]):
        kernel[z] = jnp.zeros(kernel.shape[1:], jnp.float32)


def call(kernel, shapes, operands, scratch=(), scalars=0, far=0, last=False, aliases=()):
    many = isinstance(shapes, list)
    shapes = shapes if many else [shapes]
    out = [jax.ShapeDtypeStruct(s, jnp.float32) if last else pltpu.VMEM(s, jnp.float32) for s in shapes]
    result = pl.pallas_call(
        kernel,
        out_shape=out,
        in_specs=[SMEM] * scalars + [FAR] * far + [VMEM] * (len(operands) - scalars - far),
        out_specs=[FAR] * last + [VMEM] * (len(out) - last),
        scratch_shapes=[pltpu.VMEM(s, jnp.float32) if isinstance(s, tuple) else s for s in scratch],
        compiler_params=PARAMS,
        input_output_aliases=dict(aliases),
    )(*operands)
    return result if many else result[0]


def traded(message):
    return lax.all_to_all(message, "gx", 0, 0, tiled=True)


def rotated(value, axis, by):
    count = lax.axis_size(axis)
    return lax.ppermute(value, axis, [(i, (i + by) % count) for i in range(count)])


def body(warm_start, slowness, anisotropy, observed, station_cell, source_cell):
    quakes, depth, width_x, width_y = warm_start.shape
    count_x, count_y = lax.axis_size("gx"), lax.axis_size("gy")
    index_x, index_y = lax.axis_index("gx"), lax.axis_index("gy")
    span_x, span_y = width_x * count_x, width_y * count_y
    near = 2
    per = max(1, depth // count_x)
    tile = (quakes, width_y)
    top = (width_x,) + tile
    close = (width_x, near) + tile
    field = (width_x, depth) + tile
    place = jnp.stack(
        [
            index_x * width_x,
            index_y * width_y,
            jnp.int32(span_y),
            jnp.int32(span_x * span_y),
            (index_y == 0).astype(jnp.int32),
            (index_y == count_y - 1).astype(jnp.int32),
            index_x,
            jnp.int32(span_y.bit_length() - 1),
            index_y,
        ]
    ).astype(jnp.int32)
    anis = anisotropy.reshape(3 * depth, width_x, width_y)
    local_records = observed.shape[1]
    flat = (quakes * depth * width_x, width_y)

    sources = [warm_start.reshape(quakes, depth * width_x, width_y), observed, slowness, anis]
    sources = [pltpu.with_memory_space_constraint(a, pltpu.HBM) for a in [source_cell] + sources]
    start, costs, anis, edge, to_right, to_left, records = call(
        pack_kernel,
        [field, anis.shape, (3 * near, width_x, width_y), (11 * width_x, width_y)]
        + [(6 * width_x + quakes, width_y)] * 2
        + [tile],
        [place] + sources,
        [pltpu.SMEM((quakes,), jnp.int32), (CHUNKS, quakes, depth // CHUNKS * width_x, width_y)]
        + [a.shape for a in sources[2:]]
        + [pltpu.SemaphoreType.DMA((4 + CHUNKS,))],
        scalars=1,
        far=5,
    )
    from_left = rotated(to_right, "gy", 1)
    from_right = rotated(to_left, "gy", -1)
    others = [rotated(records, "gy", by) for by in range(2, count_y - 1)]

    message_shape = (count_x, 3 * per + (8 if per > 1 else 9)) + tile
    first, first_strip, edge_costs, levels_one, sides, message = call(
        functools.partial(first_sweep_kernel, local_records, count_y, per),
        [field, (width_x, 2) + tile, (6,) + top, close, close, message_shape],
        [place, start, edge, records, from_left, from_right, costs, anis] + others,
        [(depth,) + tile, (width_x, 2) + tile],
        scalars=1,
    )
    reach = traded(message)
    chunks = -(-count_x // (width_y // 8))
    halo, *rest, message = call(
        functools.partial(middle_kernel, per, local_records * count_y),
        [(depth,) + tile, (4,) + top] + [top] * 5 + [close, close, (count_x, 2 * per + 7 + 2 * near) + tile],
        [place, station_cell.reshape(-1, width_y), reach, first, first_strip, costs, edge_costs, anis, levels_one, sides],
        [(2,) + tile, (chunks,) + tile, (chunks, depth) + tile, (width_x, 2) + tile]
        + [top] * 5
        + [(width_x, width_y), tile, tile],
        scalars=1,
    )
    times, kernel = call(
        functools.partial(last_kernel, per),
        [flat, (depth, width_x, width_y)],
        [place, traded(message), first, costs, halo] + rest + [anis],
        [field, flat, pltpu.SemaphoreType.DMA, close, (width_x, width_y), (chunks,) + tile],
        scalars=1,
        last=True,
    )
    return (times.reshape(warm_start.shape), kernel)


def solution(mesh):
    return jax.shard_map(
        body,
        mesh=mesh,
        in_specs=(
            P(None, None, "gx", "gy"),
            P(None, "gx", "gy"),
            P(None, None, "gx", "gy"),
            P(None, ("gx", "gy")),
            P(),
            P(),
        ),
        out_specs=(P(None, None, "gx", "gy"), P(None, "gx", "gy")),
        check_vma=False,
    )
```

profile of v0, /device:TPU:0, one launch (start us, length us, event | category | flops | bytes accessed | tf_op | source)
XLA Modules:
  0.0 57.4 jit_solution(18290665855367929800)
XLA Ops:
  0.6 0.1 stack.35.place
  0.7 3.0 %shard_map.77 = (f32[16,16,8,128]{3,2,1,0:T(8,128)S(1)}, f32[48,16,128]{2,1,0:T(8,128)S(1)}, f32[6,16,128]{2,1,0:T(8,128)S(1)}, f32[176,128]{1,0:T(8,128)S(1)}, ...) custom-call(s32[9]{0:T(128)S(1)} %stack.35.place, s32[8]{0:T(128)} %source_far.1, ...), custom_call_target="tpu_custom_call" | custom-call | tf_op jit(solution)/shard_map/pallas_call | solution.py:829
  3.8 0.5 collective-permute-start
  4.3 2.0 %collective-permute-start.1 = (f32[104,128]{1,0:T(8,128)S(1)}, f32[104,128]{1,0:T(8,128)S(1)}, u32[]{:S(2)}, u32[]{:S(2)}) collective-permute-start(f32[104,128]{1,0:T(8,128)S(1)} %get-tuple-element.31), channel_id=1, source_target_pairs={{0,3},{1,0},{2,1},{3,2},{4,7},{5,4},{6,5},{7,6},{8,11},{9,8},{10,9... | collective-permute-start | bytes 159752 | tf_op jit(solution)/shard_map/ppermute | solution.py:847
  6.3 2.2 %collective-permute-start.2 = (f32[8,128]{1,0:T(8,128)S(1)}, f32[8,128]{1,0:T(8,128)S(1)}, u32[]{:S(2)}, u32[]{:S(2)}) collective-permute-start(f32[8,128]{1,0:T(8,128)S(1)} %get-tuple-element.29.mine), channel_id=1, source_target_pairs={{0,2},{1,3},{2,0},{3,1},{4,6},{5,7},{6,4},{7,5},{8,10},{9,11},{10,... | collective-permute-start | bytes 12296 | tf_op jit(solution)/shard_map/ppermute | solution.py:847
  8.5 2.2 %collective-permute-done.2.rest_0_ = f32[8,128]{1,0:T(8,128)S(1)} collective-permute-done((f32[8,128]{1,0:T(8,128)S(1)}, f32[8,128]{1,0:T(8,128)S(1)}, u32[]{:S(2)}, u32[]{:S(2)}) %collective-permute-start.2) | collective-permute-done | bytes 4128 | tf_op jit(solution)/shard_map/ppermute | solution.py:847
  10.6 0.0 collective-permute-done.from_left
  10.7 0.0 collective-permute-done.1.from_right
  10.7 4.1 %shard_map.78 = (f32[16,16,8,128]{3,2,1,0:T(8,128)S(1)}, f32[16,2,8,128]{3,2,1,0:T(8,128)S(1)}, f32[6,16,8,128]{3,2,1,0:T(8,128)S(1)}, f32[16,2,8,128]{3,2,1,0:T...) custom-call(s32[9]{0:T(128)S(1)} %stack.35.place, ...), custom_call_target="tpu_custom_call" | custom-call | tf_op jit(solution)/shard_map/pallas_call | solution.py:829
  14.8 18.8 %all_to_all.10.received = f32[8,14,8,128]{3,2,1,0:T(8,128)S(1)} all-to-all(f32[8,14,8,128]{3,2,1,0:T(8,128)S(1)} %get-tuple-element.34), channel_id=1, replica_groups=mesh['gx'=8,'gy'=4] {'gx'}, dimensions={0} | all-to-all | bytes 917504 | tf_op jit(solution)/shard_map/all_to_all | solution.py:842
  33.6 0.0 copy-start
  33.6 0.7 %copy-done = s32[512]{0:T(512)S(1)} copy-done((s32[512]{0:T(512)S(1)}, s32[512]{0:T(512)}, u32[]{:S(2)}) %copy-start) | copy-done | bytes 2072
  34.3 2.0 %shard_map.79 = (f32[16,8,128]{2,1,0:T(8,128)S(1)}, f32[4,16,8,128]{3,2,1,0:T(8,128)S(1)}, f32[16,8,128]{2,1,0:T(8,128)S(1)}, f32[16,8,128]{2,1,0:T(8,128)S(1)},...) custom-call(s32[9]{0:T(128)S(1)} %stack.35.place, ...), custom_call_target="tpu_custom_call" | custom-call | tf_op jit(solution)/shard_map/pallas_call | solution.py:829
  36.3 16.8 %all_to_all.11.received = f32[8,15,8,128]{3,2,1,0:T(8,128)S(1)} all-to-all(f32[8,15,8,128]{3,2,1,0:T(8,128)S(1)} %get-tuple-element.40), channel_id=1, replica_groups=mesh['gx'=8,'gy'=4] {'gx'}, dimensions={0} | all-to-all | bytes 983040 | tf_op jit(solution)/shard_map/all_to_all | solution.py:842
  53.1 4.3 %shard_map.80 = (f32[2048,128]{1,0:T(8,128)}, f32[16,16,128]{2,1,0:T(8,128)}) custom-call(s32[9]{0:T(128)S(1)} %stack.35.place, f32[8,15,8,128]{3,2,1,0:T(8,128)S(1)} %all_to_all.11.received, f32[16,16,8,128]{3,2,1,0:T(8,128)S(1)} %get-tuple-element.35.first, f32[48,16,128]{2,1,0:T(8,128)S(1)} %get-tuple-element.32.costs, ...), custom_call_target="tpu_custom_call" | custom-call | tf_op jit(solution)/shard_map/pallas_call | solution.py:829
Async XLA Ops:
  3.8 6.9 %collective-permute-start = (f32[104,128]{1,0:T(8,128)S(1)}, f32[104,128]{1,0:T(8,128)S(1)}, u32[]{:S(2)}, u32[]{:S(2)}) collective-permute-start(f32[104,128]{1,0:T(8,128)S(1)} %get-tuple-element.30), channel_id=1, source_target_pairs={{0,1},{1,2},{2,3},{3,0},{4,5},{5,6},{6,7},{7,4},{8,9},{9,10},{10,1... | collective-permute-start | bytes 159752 | tf_op jit(solution)/shard_map/ppermute | solution.py:847
  4.3 6.4 %collective-permute-start.1 = (f32[104,128]{1,0:T(8,128)S(1)}, f32[104,128]{1,0:T(8,128)S(1)}, u32[]{:S(2)}, u32[]{:S(2)}) collective-permute-start(f32[104,128]{1,0:T(8,128)S(1)} %get-tuple-element.31), channel_id=1, source_target_pairs={{0,3},{1,0},{2,1},{3,2},{4,7},{5,4},{6,5},{7,6},{8,11},{9,8},{10,9... | collective-permute-start | bytes 159752 | tf_op jit(solution)/shard_map/ppermute | solution.py:847
  6.3 4.4 %collective-permute-start.2 = (f32[8,128]{1,0:T(8,128)S(1)}, f32[8,128]{1,0:T(8,128)S(1)}, u32[]{:S(2)}, u32[]{:S(2)}) collective-permute-start(f32[8,128]{1,0:T(8,128)S(1)} %get-tuple-element.29.mine), channel_id=1, source_target_pairs={{0,2},{1,3},{2,0},{3,1},{4,6},{5,7},{6,4},{7,5},{8,10},{9,11},{10,... | collective-permute-start | bytes 12296 | tf_op jit(solution)/shard_map/ppermute | solution.py:847
  33.6 0.7 %copy-start = (s32[512]{0:T(512)S(1)}, s32[512]{0:T(512)}, u32[]{:S(2)}) copy-start(s32[512]{0:T(512)} %param.10) | copy-start | bytes 6148
where the time goes:
time: 57.7 us; the launch traced here: 57.4 us
  blocking collectives  35.6 us (62%)
  Pallas kernels  13.5 us (23%)
  starting transfers between devices  4.74 us (8%)
  waiting for transfers between devices  2.16 us (4%)
  local copies, waits for them, and re-layouts  0.77 us (1%)
  between operations  0.66 us (1%)
    all_to_all x2, blocking collectives, traded(): return lax.all_to_all(message, 'gx', 0, 0, tiled=True)  35.6 us
    pallas_call x4, Pallas kernels, call(): pl.pallas_call(kernel, out_shape=out, in_specs=[SMEM] * scalars + [FAR] *...  13.5 us
    ppermute x3, starting transfers between devices, rotated(): lax.ppermute(value, axis, [(i, (i + by) % count) for i in range(count)])  4.74 us
    ppermute x3, waiting for transfers between devices, rotated(): lax.ppermute(value, axis, [(i, (i + by) % count) for i in range(count)])  2.16 us
  transfers between devices with their start and end apart: 3, of which 1 were waited for; matrix products, arithmetic and copies ran while one was open for 0% of the time, Pallas kernels for 0%

commit v1 on v0

--- a/solution.py
+++ b/solution.py
@@ -100,14 +100,15 @@
 
 
 def pack_kernel(
-    place, source_far, warm_far, observed_far, slowness_far, anisotropy_far, start, costs, near, edge, to_right, to_left, records,
+    place, source_far, warm_far, observed_far, slowness_far, anisotropy_far, stations_far,
+    start, costs, near, edge, to_right, to_left, records, stations,
     source, warm, observed, slowness, anisotropy, arrived,
 ):
     pairs = [(slowness_far, slowness), (anisotropy_far, anisotropy), (observed_far, observed)]
     share = start.shape[1] // CHUNKS
     span = share * start.shape[0]
     pairs += [(warm_far.at[:, pl.ds(i * span, span)], warm.at[i]) for i in range(CHUNKS)]
-    pairs += [(source_far, source)]
+    pairs += [(stations_far, stations), (source_far, source)]
     copies = [pltpu.make_async_copy(a, b, arrived.at[i]) for i, (a, b) in enumerate(pairs)]
     for copy in copies:
         copy.start()
@@ -168,6 +169,7 @@
         to_right[4 * x : 4 * x + 8, :] = jnp.where(low, one, pltpu.roll(two, 4, 0))
         to_left[4 * x : 4 * x + 8, :] = jnp.where(low, pltpu.roll(one, 4, 0), two)
     copies[2].wait()
+    copies[-2].wait()
     records[...] = jnp.zeros(tile, jnp.float32)
     records[:, : observed.shape[1]] = observed[...]
     for message in (to_right, to_left):
@@ -268,6 +270,33 @@
         paths.append(jnp.where(lane >= shape[1] - 8, BIG, pltpu.roll(sums, shape[1] - 8, 1) + step_z))
         totals = [t + jnp.exp2(-p) for t, p in zip(totals, paths)]
     return sums, [-LOG2E * jnp.log(jnp.maximum(t, 1e-37)) for t in totals]
+
+
+PLACES = ((2, 0, 16), (4, 16, 16), (5, 32, 16), (7, 48, 16))
+BACK_PLACES = ((3, 64, 8), (6, 72, 8))
+
+
+def shared_tile(reach, back, records):
+    lane, sub = iota(reach.shape, 1), iota(reach.shape, 0)
+    extra = reach
+    for value, places in ((reach, PLACES), (back, BACK_PLACES)):
+        for at, low, width in places:
+            moved = pltpu.roll(pltpu.roll(value, (2 - at) % 8, 0), low, 1) if low else value
+            extra = jnp.where((lane >= low) & (lane < low + width), moved, extra)
+    half = reach.shape[1] // 2
+    record = jnp.where(lane < half, pltpu.roll(records, 4, 0), pltpu.roll(records, half, 1))
+    tile = jnp.where(sub == 0, shifted_down(reach, 3), jnp.where(sub == 1, shifted_down(reach, 5), extra))
+    return jnp.where(sub < 4, tile, record)
+
+
+def unshared_tile(tile):
+    sub = iota(tile.shape, 0)
+    wide = tile.shape[1]
+    reach = jnp.where(sub == 3, pltpu.roll(tile, 3, 0), jnp.where(sub == 6, pltpu.roll(tile, 5, 0), tile))
+    for at, low, _ in PLACES[1:]:
+        reach = jnp.where(sub == at, pltpu.roll(pltpu.roll(tile, at - 2, 0), wide - low, 1), reach)
+    back = [pltpu.roll(pltpu.roll(tile, at - 2, 0), wide - low, 1) for at, low, _ in BACK_PLACES]
+    return reach, jnp.where(sub == 3, back[0], back[1])
 
 
 def shared_rows(total, paths):
@@ -423,9 +452,7 @@
     tiles = passages(costs, left_costs[0], right_costs[0], depth)
     strip_total, strip_paths = strip_passages(edge_costs, width_x)
 
-    back_strip = packed(*back_strips)
-    reach_strip = jnp.where(sub == 0, shifted_down(back_strip, 3), reach_strip)
-    reach_strip = jnp.where(sub == 1, shifted_down(back_strip, 5), reach_strip)
+    strip_tile = shared_tile(reach_strip, packed(*back_strips), records)
     shared = shared_rows(strip_total, strip_paths)
     count = message.shape[0]
     for p in range(count):
@@ -443,10 +470,9 @@
             if per > 1 and k == 1:
                 value = jnp.where(sub < 6, value, shared)
             message[p, 2 * per + 2 + k] = value
-        message[p, 3 * per + 2] = reach_strip
-        message[p, 3 * per + 3] = records
+        message[p, 3 * per + 2] = strip_tile
         if per == 1:
-            message[p, 3 * per + 4] = shared
+            message[p, 3 * per + 3] = shared
         surface = [state[0], state[1], back[0], jnp.where(sub < 6, tiles[0], jnp.broadcast_to(tiles[1][:1], tile))]
         for i, value in enumerate(surface):
             message[p, message.shape[1] - 4 + i] = value
@@ -475,7 +501,8 @@
     def further(pair, cost):
         return pair[0] + cost, pair[1]
 
-    shared = [received[d, 2 * per + 3] if per > 1 else received[d, 3 * per + 4] for d in range(count)]
+    shared = [received[d, 2 * per + 3] if per > 1 else received[d, 3 * per + 3] for d in range(count)]
+    strips = [unshared_tile(received[d, side]) for d in range(count)]
     shared = spread_rows(shared)
     state = [(blank, unit)] * (per + 2)
     strip = (blank, unit)
@@ -486,7 +513,7 @@
         state = [
             join_pairs((received[device, k], unit), further(state[k], total(device, k - 1))) for k in range(per + 2)
         ]
-        strip = join_pairs((received[device, side], unit), further(strip, shared[device][0]))
+        strip = join_pairs((strips[device][0], unit), further(strip, shared[device][0]))
     own = blank
     for device in range(count):
         own = jnp.where(device == me, first_strip[device], own)
@@ -518,8 +545,7 @@
             least, _, amount = softmin(values)
             state[k] = join_pairs((least, amount), further(state[k], total(device, k)))
         u = first_strip[device]
-        back = received[device, side]
-        back = jnp.where(iota(tile, 0) == 3, pltpu.roll(back, 3, 0), pltpu.roll(back, 5, 0))
+        back = strips[device][1]
         paths = shared[device][1]
         values = [back, u + paths[0], pltpu.roll(u, 1, 0) + paths[1], shifted_down(u, 1) + paths[2]]
         values.append(jnp.where(lane < 8, BIG, pltpu.roll(u, 8, 1)) + paths[3])
@@ -542,7 +568,7 @@
     count = received.shape[0]
     base = received.shape[1] - 4
     me = place[6]
-    add_records(rows_of, 3 * per + 3, place, cell, received, sums, counts, sums_strip, counts_strip)
+    add_records(rows_of, 3 * per + 2, place, cell, received, sums, counts, sums_strip, counts_strip)
     blank = jnp.full(tile, BIG, jnp.float32)
     unit = jnp.ones(tile, jnp.float32)
 
@@ -685,6 +711,7 @@
         records = jnp.zeros((quakes, width_y), jnp.float32)
         for part in range(share):
             piece = received[chunk * share + part, last]
+            piece = jnp.where(iota(piece.shape, 0) < 4, pltpu.roll(piece, 4, 0), pltpu.roll(piece, width_y // 2, 1))
             moved = pltpu.roll(piece, part * rows_of, 1) if part else piece
             records = jnp.where(lane // rows_of == part, moved, records)
         cells = cell[chunk : chunk + 1, :]
@@ -825,7 +852,8 @@
 def call(kernel, shapes, operands, scratch=(), scalars=0, far=0, last=False, aliases=()):
     many = isinstance(shapes, list)
     shapes = shapes if many else [shapes]
-    out = [jax.ShapeDtypeStruct(s, jnp.float32) if last else pltpu.VMEM(s, jnp.float32) for s in shapes]
+    held = jax.ShapeDtypeStruct if last else pltpu.VMEM
+    out = [held(s, jnp.float32) if isinstance(s, tuple) else s for s in shapes]
     result = pl.pallas_call(
         kernel,
         out_shape=out,
@@ -875,25 +903,26 @@
     local_records = observed.shape[1]
     flat = (quakes * depth * width_x, width_y)
 
-    sources = [warm_start.reshape(quakes, depth * width_x, width_y), observed, slowness, anis]
+    stations = station_cell.reshape(-1, width_y)
+    sources = [warm_start.reshape(quakes, depth * width_x, width_y), observed, slowness, anis, stations]
     sources = [pltpu.with_memory_space_constraint(a, pltpu.HBM) for a in [source_cell] + sources]
-    start, costs, anis, edge, to_right, to_left, records = call(
+    start, costs, anis, edge, to_right, to_left, records, stations = call(
         pack_kernel,
         [field, anis.shape, (3 * near, width_x, width_y), (11 * width_x, width_y)]
         + [(6 * width_x + quakes, width_y)] * 2
-        + [tile],
+        + [tile, pltpu.VMEM(stations.shape, jnp.int32)],
         [place] + sources,
         [pltpu.SMEM((quakes,), jnp.int32), (CHUNKS, quakes, depth // CHUNKS * width_x, width_y)]
-        + [a.shape for a in sources[2:]]
-        + [pltpu.SemaphoreType.DMA((4 + CHUNKS,))],
+        + [a.shape for a in sources[2:5]]
+        + [pltpu.SemaphoreType.DMA((5 + CHUNKS,))],
         scalars=1,
-        far=5,
+        far=6,
     )
     from_left = rotated(to_right, "gy", 1)
     from_right = rotated(to_left, "gy", -1)
     others = [rotated(records, "gy", by) for by in range(2, count_y - 1)]
 
-    message_shape = (count_x, 3 * per + (8 if per > 1 else 9)) + tile
+    message_shape = (count_x, 3 * per + (7 if per > 1 else 8)) + tile
     first, first_strip, edge_costs, levels_one, sides, message = call(
         functools.partial(first_sweep_kernel, local_records, count_y, per),
         [field, (width_x, 2) + tile, (6,) + top, close, close, message_shape],
@@ -906,7 +935,7 @@
     halo, *rest, message = call(
         functools.partial(middle_kernel, per, local_records * count_y),
         [(depth,) + tile, (4,) + top] + [top] * 5 + [close, close, (count_x, 2 * per + 7 + 2 * near) + tile],
-        [place, station_cell.reshape(-1, width_y), reach, first, first_strip, costs, edge_costs, anis, levels_one, sides],
+        [place, stations, reach, first, first_strip, costs, edge_costs, anis, levels_one, sides],
         [(2,) + tile, (chunks,) + tile, (chunks, depth) + tile, (width_x, 2) + tile]
         + [top] * 5
         + [(width_x, width_y), tile, tile],

time: 57.7 us -> 56.4 us (0.977)
  local copies, waits for them, and re-layouts: 0.77 us -> 0.09 us
  blocking collectives: 35.6 us -> 35 us
    unnamed x2 -> x0, local copies, waits for them, and re-layouts: 0.68 us -> none
    all_to_all x2, blocking collectives: 35.6 us -> 35 us  [traded(): return lax.all_to_all(message, 'gx', 0, 0, tiled=True)]
where the time goes in v1:
time: 56.4 us; the launch traced here: 56.2 us
  blocking collectives  35 us (62%)
  Pallas kernels  13.6 us (24%)
  starting transfers between devices  4.74 us (8%)
  waiting for transfers between devices  2.16 us (4%)
  between operations  0.66 us (1%)
    all_to_all x2, blocking collectives, traded(): return lax.all_to_all(message, 'gx', 0, 0, tiled=True)  35 us
    pallas_call x4, Pallas kernels, call(): pl.pallas_call(kernel, out_shape=out, in_specs=[SMEM] * scalars + [FAR] *...  13.6 us
    ppermute x3, starting transfers between devices, rotated(): lax.ppermute(value, axis, [(i, (i + by) % count) for i in range(count)])  4.74 us
    ppermute x3, waiting for transfers between devices, rotated(): lax.ppermute(value, axis, [(i, (i + by) % count) for i in range(count)])  2.16 us
  transfers between devices with their start and end apart: 3, of which 1 were waited for; matrix products, arithmetic and copies ran while one was open for 0% of the time, Pallas kernels for 0%

profile of v1, /device:TPU:0, one launch (start us, length us, event | category | flops | bytes accessed | tf_op | source)
XLA Modules:
  0.0 56.2 jit_solution(15523078618908321357)
XLA Ops:
  0.6 0.1 stack.35.place
  0.7 3.0 %shard_map.77 = (f32[16,16,8,128]{3,2,1,0:T(8,128)S(1)}, f32[48,16,128]{2,1,0:T(8,128)S(1)}, f32[6,16,128]{2,1,0:T(8,128)S(1)}, f32[176,128]{1,0:T(8,128)S(1)}, ...) custom-call(s32[9]{0:T(128)S(1)} %stack.35.place, s32[8]{0:T(128)} %source_far.1, ...), custom_call_target="tpu_custom_call" | custom-call | tf_op jit(solution)/shard_map/pallas_call | solution.py:857
  3.8 0.5 collective-permute-start
  4.3 2.0 %collective-permute-start.1 = (f32[104,128]{1,0:T(8,128)S(1)}, f32[104,128]{1,0:T(8,128)S(1)}, u32[]{:S(2)}, u32[]{:S(2)}) collective-permute-start(f32[104,128]{1,0:T(8,128)S(1)} %get-tuple-element.33), channel_id=1, source_target_pairs={{0,3},{1,0},{2,1},{3,2},{4,7},{5,4},{6,5},{7,6},{8,11},{9,8},{10,9... | collective-permute-start | bytes 159752 | tf_op jit(solution)/shard_map/ppermute | solution.py:875
  6.3 2.2 %collective-permute-start.2 = (f32[8,128]{1,0:T(8,128)S(1)}, f32[8,128]{1,0:T(8,128)S(1)}, u32[]{:S(2)}, u32[]{:S(2)}) collective-permute-start(f32[8,128]{1,0:T(8,128)S(1)} %get-tuple-element.31.mine), channel_id=1, source_target_pairs={{0,2},{1,3},{2,0},{3,1},{4,6},{5,7},{6,4},{7,5},{8,10},{9,11},{10,... | collective-permute-start | bytes 12296 | tf_op jit(solution)/shard_map/ppermute | solution.py:875
  8.5 2.2 %collective-permute-done.2.rest_0_ = f32[8,128]{1,0:T(8,128)S(1)} collective-permute-done((f32[8,128]{1,0:T(8,128)S(1)}, f32[8,128]{1,0:T(8,128)S(1)}, u32[]{:S(2)}, u32[]{:S(2)}) %collective-permute-start.2) | collective-permute-done | bytes 4128 | tf_op jit(solution)/shard_map/ppermute | solution.py:875
  10.7 0.0 collective-permute-done.from_left
  10.7 0.0 collective-permute-done.1.from_right
  10.7 4.2 %shard_map.78 = (f32[16,16,8,128]{3,2,1,0:T(8,128)S(1)}, f32[16,2,8,128]{3,2,1,0:T(8,128)S(1)}, f32[6,16,8,128]{3,2,1,0:T(8,128)S(1)}, f32[16,2,8,128]{3,2,1,0:T...) custom-call(s32[9]{0:T(128)S(1)} %stack.35.place, ...), custom_call_target="tpu_custom_call" | custom-call | tf_op jit(solution)/shard_map/pallas_call | solution.py:857
  14.8 18.2 %all_to_all.10.received = f32[8,13,8,128]{3,2,1,0:T(8,128)S(1)} all-to-all(f32[8,13,8,128]{3,2,1,0:T(8,128)S(1)} %get-tuple-element.36), channel_id=1, replica_groups=mesh['gx'=8,'gy'=4] {'gx'}, dimensions={0} | all-to-all | bytes 851968 | tf_op jit(solution)/shard_map/all_to_all | solution.py:870
  33.1 2.1 %shard_map.79 = (f32[16,8,128]{2,1,0:T(8,128)S(1)}, f32[4,16,8,128]{3,2,1,0:T(8,128)S(1)}, f32[16,8,128]{2,1,0:T(8,128)S(1)}, f32[16,8,128]{2,1,0:T(8,128)S(1)},...) custom-call(s32[9]{0:T(128)S(1)} %stack.35.place, ...), custom_call_target="tpu_custom_call" | custom-call | tf_op jit(solution)/shard_map/pallas_call | solution.py:857
  35.1 16.7 %all_to_all.11.received = f32[8,15,8,128]{3,2,1,0:T(8,128)S(1)} all-to-all(f32[8,15,8,128]{3,2,1,0:T(8,128)S(1)} %get-tuple-element.42), channel_id=1, replica_groups=mesh['gx'=8,'gy'=4] {'gx'}, dimensions={0} | all-to-all | bytes 983040 | tf_op jit(solution)/shard_map/all_to_all | solution.py:870
  51.9 4.3 %shard_map.80 = (f32[2048,128]{1,0:T(8,128)}, f32[16,16,128]{2,1,0:T(8,128)}) custom-call(s32[9]{0:T(128)S(1)} %stack.35.place, f32[8,15,8,128]{3,2,1,0:T(8,128)S(1)} %all_to_all.11.received, f32[16,16,8,128]{3,2,1,0:T(8,128)S(1)} %get-tuple-element.37.first, f32[48,16,128]{2,1,0:T(8,128)S(1)} %get-tuple-element.34.costs, ...), custom_call_target="tpu_custom_call" | custom-call | tf_op jit(solution)/shard_map/pallas_call | solution.py:857
Async XLA Ops:
  3.8 6.9 %collective-permute-start = (f32[104,128]{1,0:T(8,128)S(1)}, f32[104,128]{1,0:T(8,128)S(1)}, u32[]{:S(2)}, u32[]{:S(2)}) collective-permute-start(f32[104,128]{1,0:T(8,128)S(1)} %get-tuple-element.32), channel_id=1, source_target_pairs={{0,1},{1,2},{2,3},{3,0},{4,5},{5,6},{6,7},{7,4},{8,9},{9,10},{10,1... | collective-permute-start | bytes 159752 | tf_op jit(solution)/shard_map/ppermute | solution.py:875
  4.3 6.4 %collective-permute-start.1 = (f32[104,128]{1,0:T(8,128)S(1)}, f32[104,128]{1,0:T(8,128)S(1)}, u32[]{:S(2)}, u32[]{:S(2)}) collective-permute-start(f32[104,128]{1,0:T(8,128)S(1)} %get-tuple-element.33), channel_id=1, source_target_pairs={{0,3},{1,0},{2,1},{3,2},{4,7},{5,4},{6,5},{7,6},{8,11},{9,8},{10,9... | collective-permute-start | bytes 159752 | tf_op jit(solution)/shard_map/ppermute | solution.py:875
  6.3 4.4 %collective-permute-start.2 = (f32[8,128]{1,0:T(8,128)S(1)}, f32[8,128]{1,0:T(8,128)S(1)}, u32[]{:S(2)}, u32[]{:S(2)}) collective-permute-start(f32[8,128]{1,0:T(8,128)S(1)} %get-tuple-element.31.mine), channel_id=1, source_target_pairs={{0,2},{1,3},{2,0},{3,1},{4,6},{5,7},{6,4},{7,5},{8,10},{9,11},{10,... | collective-permute-start | bytes 12296 | tf_op jit(solution)/shard_map/ppermute | solution.py:875

commit v2 on v1

--- a/solution.py
+++ b/solution.py
@@ -102,17 +102,18 @@
 def pack_kernel(
     place, source_far, warm_far, observed_far, slowness_far, anisotropy_far, stations_far,
     start, costs, near, edge, to_right, to_left, records, stations,
-    source, warm, observed, slowness, anisotropy, arrived,
+    source, observed, slowness, anisotropy, arrived,
 ):
     pairs = [(slowness_far, slowness), (anisotropy_far, anisotropy), (observed_far, observed)]
-    share = start.shape[1] // CHUNKS
-    span = share * start.shape[0]
-    pairs += [(warm_far.at[:, pl.ds(i * span, span)], warm.at[i]) for i in range(CHUNKS)]
     pairs += [(stations_far, stations), (source_far, source)]
+    depth, width_x, quakes, width_y = start.shape
+    share = depth // CHUNKS
+    for i in range(CHUNKS):
+        levels = pl.ds(i * share, share)
+        pairs += [(warm_far.at[e, levels], start.at[levels, :, e, :]) for e in range(quakes)]
     copies = [pltpu.make_async_copy(a, b, arrived.at[i]) for i, (a, b) in enumerate(pairs)]
     for copy in copies:
         copy.start()
-    width_x, depth, quakes, width_y = start.shape
     tile = (quakes, width_y)
     quake = iota(tile, 0)
     lane = iota(tile, 1)
@@ -142,23 +143,23 @@
     at = slice(5 * width_x, 6 * width_x)
     to_right[at, :] = native[2]
     to_left[at, :] = native[2]
-    copies[-1].wait()
+    copies[4].wait()
     cell = jnp.zeros(tile, jnp.int32)
     for e in range(quakes):
         cell = jnp.where(quake == e, source[e], cell)
     cell = cell - (lane + place[0] * span_y + place[1])
     edges = []
     for i in range(CHUNKS):
-        copies[3 + i].wait()
-        here = warm.at[i].reshape(quakes * share * width_x, width_y)
+        for copy in copies[5 + i * quakes : 5 + (i + 1) * quakes]:
+            copy.wait()
 
         chunk = [jnp.zeros(tile, jnp.float32)] * share
         for x in range(width_x):
             mine = (lane >> 3) == x
             for k in range(share):
-                value = here[pl.ds(k * width_x + x, quakes, stride=share * width_x), :] * RATE
+                value = start[i * share + k, x] * RATE
                 value = jnp.where(cell == (i * share + k) * plane + x * span_y, 0.0, value)
-                start[x, i * share + k] = value
+                start[i * share + k, x] = value
                 chunk[k] = jnp.where(mine, pltpu.roll(value, (8 * x + 4) % width_y, 1), chunk[k])
         edges += chunk
     columns = jnp.transpose(jnp.concatenate(edges, 0))
@@ -169,7 +170,7 @@
         to_right[4 * x : 4 * x + 8, :] = jnp.where(low, one, pltpu.roll(two, 4, 0))
         to_left[4 * x : 4 * x + 8, :] = jnp.where(low, pltpu.roll(one, 4, 0), two)
     copies[2].wait()
-    copies[-2].wait()
+    copies[3].wait()
     records[...] = jnp.zeros(tile, jnp.float32)
     records[:, : observed.shape[1]] = observed[...]
     for message in (to_right, to_left):
@@ -390,7 +391,7 @@
 ):
     others = rest[: count_y - 3]
     local, local_strip, edge_costs, levels, sides, message, halo, strip = rest[count_y - 3 :]
-    width_x, depth, quakes, width_y = field.shape
+    depth, width_x, quakes, width_y = field.shape
     tile = (quakes, width_y)
     sub = iota(tile, 0)
     low = sub < 4
@@ -429,7 +430,7 @@
         sides[x, z] = sideways + row(anisotropy, 2 * near + z, x, tile) * vertical
 
     def step(x, carry):
-        state, strips = sweep_step(x, near, [field[x, z] for z in range(depth)], strip, costs, edge_costs, halo, *carry, keep, None)
+        state, strips = sweep_step(x, near, [field[z, x] for z in range(depth)], strip, costs, edge_costs, halo, *carry, keep, None)
         for z in range(depth):
             local[x, z] = state[z]
         for side in range(2):
@@ -764,7 +765,7 @@
         values = [field[x, z] for z in range(depth)]
         state, _ = sweep_step(x, 0, values, None, costs, None, halo, state, None, None, None)
         for z in range(depth):
-            times[pl.ds(z * width_x + x, quakes, stride=depth * width_x), :] = state[z] * (1.0 / RATE)
+            times[z, x] = state[z] * (1.0 / RATE)
         return state
 
     all_steps(width_x, step, carried[1])
@@ -775,13 +776,15 @@
     gains, anisotropy, times, kernel, field, value, copied, entries, top, sent,
 ):
     traveltimes(per, first, received, costs, halo, value, field)
-    copy = pltpu.make_async_copy(value, times, copied)
-    copy.start()
+    copies = [pltpu.make_async_copy(value.at[:, :, e, :], times.at[e], copied.at[e]) for e in range(times.shape[0])]
+    for copy in copies:
+        copy.start()
     adjoint(
         2 * per, place, received, shares, slopes, keeps, misfits, edges_own, edges_factor, slopes_one, gains, anisotropy,
         kernel, entries, top, sent,
     )
-    copy.wait()
+    for copy in copies:
+        copy.wait()
 
 
 def adjoint(
@@ -901,20 +904,19 @@
     ).astype(jnp.int32)
     anis = anisotropy.reshape(3 * depth, width_x, width_y)
     local_records = observed.shape[1]
-    flat = (quakes * depth * width_x, width_y)
 
     stations = station_cell.reshape(-1, width_y)
-    sources = [warm_start.reshape(quakes, depth * width_x, width_y), observed, slowness, anis, stations]
+    sources = [warm_start, observed, slowness, anis, stations]
     sources = [pltpu.with_memory_space_constraint(a, pltpu.HBM) for a in [source_cell] + sources]
     start, costs, anis, edge, to_right, to_left, records, stations = call(
         pack_kernel,
-        [field, anis.shape, (3 * near, width_x, width_y), (11 * width_x, width_y)]
+        [(depth, width_x) + tile, anis.shape, (3 * near, width_x, width_y), (11 * width_x, width_y)]
         + [(6 * width_x + quakes, width_y)] * 2
         + [tile, pltpu.VMEM(stations.shape, jnp.int32)],
         [place] + sources,
-        [pltpu.SMEM((quakes,), jnp.int32), (CHUNKS, quakes, depth // CHUNKS * width_x, width_y)]
+        [pltpu.SMEM((quakes,), jnp.int32)]
         + [a.shape for a in sources[2:5]]
-        + [pltpu.SemaphoreType.DMA((5 + CHUNKS,))],
+        + [pltpu.SemaphoreType.DMA((5 + CHUNKS * quakes,))],
         scalars=1,
         far=6,
     )
@@ -943,13 +945,13 @@
     )
     times, kernel = call(
         functools.partial(last_kernel, per),
-        [flat, (depth, width_x, width_y)],
+        [warm_start.shape, (depth, width_x, width_y)],
         [place, traded(message), first, costs, halo] + rest + [anis],
-        [field, flat, pltpu.SemaphoreType.DMA, close, (width_x, width_y), (chunks,) + tile],
+        [field, (depth, width_x) + tile, pltpu.SemaphoreType.DMA((quakes,)), close, (width_x, width_y), (chunks,) + tile],
         scalars=1,
         last=True,
     )
-    return (times.reshape(warm_start.shape), kernel)
+    return (times, kernel)
 
 
 def solution(mesh):

time: 56.4 us -> 56 us (level)
  no operation moved by 1% of the time
where the time goes in v2:
time: 56 us; the launch traced here: 55.8 us
  blocking collectives  35 us (62%)
  Pallas kernels  13.2 us (24%)
  starting transfers between devices  4.74 us (8%)
  waiting for transfers between devices  2.16 us (4%)
  between operations  0.66 us (1%)
    all_to_all x2, blocking collectives, traded(): return lax.all_to_all(message, 'gx', 0, 0, tiled=True)  35 us
    pallas_call x4, Pallas kernels, call(): pl.pallas_call(kernel, out_shape=out, in_specs=[SMEM] * scalars + [FAR] *...  13.2 us
    ppermute x3, starting transfers between devices, rotated(): lax.ppermute(value, axis, [(i, (i + by) % count) for i in range(count)])  4.74 us
    ppermute x3, waiting for transfers between devices, rotated(): lax.ppermute(value, axis, [(i, (i + by) % count) for i in range(count)])  2.16 us
  transfers between devices with their start and end apart: 3, of which 1 were waited for; matrix products, arithmetic and copies ran while one was open for 0% of the time, Pallas kernels for 0%

profile of v2, /device:TPU:0, one launch (start us, length us, event | category | flops | bytes accessed | tf_op | source)
XLA Modules:
  0.0 55.8 jit_solution(9968849390946695789)
XLA Ops:
  0.6 0.1 stack.35.place
  0.7 2.9 %shard_map.77 = (f32[16,16,8,128]{3,2,1,0:T(8,128)S(1)}, f32[48,16,128]{2,1,0:T(8,128)S(1)}, f32[6,16,128]{2,1,0:T(8,128)S(1)}, f32[176,128]{1,0:T(8,128)S(1)}, ...) custom-call(s32[9]{0:T(128)S(1)} %stack.35.place, s32[8]{0:T(128)} %source_far.1, ...), custom_call_target="tpu_custom_call" | custom-call | tf_op jit(solution)/shard_map/pallas_call | solution.py:860
  3.6 0.5 collective-permute-start
  4.1 2.0 %collective-permute-start.1 = (f32[104,128]{1,0:T(8,128)S(1)}, f32[104,128]{1,0:T(8,128)S(1)}, u32[]{:S(2)}, u32[]{:S(2)}) collective-permute-start(f32[104,128]{1,0:T(8,128)S(1)} %get-tuple-element.31), channel_id=1, source_target_pairs={{0,3},{1,0},{2,1},{3,2},{4,7},{5,4},{6,5},{7,6},{8,11},{9,8},{10,9... | collective-permute-start | bytes 159752 | tf_op jit(solution)/shard_map/ppermute | solution.py:878
  6.1 2.2 %collective-permute-start.2 = (f32[8,128]{1,0:T(8,128)S(1)}, f32[8,128]{1,0:T(8,128)S(1)}, u32[]{:S(2)}, u32[]{:S(2)}) collective-permute-start(f32[8,128]{1,0:T(8,128)S(1)} %get-tuple-element.29.mine), channel_id=1, source_target_pairs={{0,2},{1,3},{2,0},{3,1},{4,6},{5,7},{6,4},{7,5},{8,10},{9,11},{10,... | collective-permute-start | bytes 12296 | tf_op jit(solution)/shard_map/ppermute | solution.py:878
  8.3 2.2 %collective-permute-done.2.rest_0_ = f32[8,128]{1,0:T(8,128)S(1)} collective-permute-done((f32[8,128]{1,0:T(8,128)S(1)}, f32[8,128]{1,0:T(8,128)S(1)}, u32[]{:S(2)}, u32[]{:S(2)}) %collective-permute-start.2) | collective-permute-done | bytes 4128 | tf_op jit(solution)/shard_map/ppermute | solution.py:878
  10.5 0.0 collective-permute-done.from_left
  10.5 0.0 collective-permute-done.1.from_right
  10.5 4.2 %shard_map.78 = (f32[16,16,8,128]{3,2,1,0:T(8,128)S(1)}, f32[16,2,8,128]{3,2,1,0:T(8,128)S(1)}, f32[6,16,8,128]{3,2,1,0:T(8,128)S(1)}, f32[16,2,8,128]{3,2,1,0:T...) custom-call(s32[9]{0:T(128)S(1)} %stack.35.place, ...), custom_call_target="tpu_custom_call" | custom-call | tf_op jit(solution)/shard_map/pallas_call | solution.py:860
  14.7 18.2 %all_to_all.10.received = f32[8,13,8,128]{3,2,1,0:T(8,128)S(1)} all-to-all(f32[8,13,8,128]{3,2,1,0:T(8,128)S(1)} %get-tuple-element.34), channel_id=1, replica_groups=mesh['gx'=8,'gy'=4] {'gx'}, dimensions={0} | all-to-all | bytes 851968 | tf_op jit(solution)/shard_map/all_to_all | solution.py:873
  32.9 2.1 %shard_map.79 = (f32[16,8,128]{2,1,0:T(8,128)S(1)}, f32[4,16,8,128]{3,2,1,0:T(8,128)S(1)}, f32[16,8,128]{2,1,0:T(8,128)S(1)}, f32[16,8,128]{2,1,0:T(8,128)S(1)},...) custom-call(s32[9]{0:T(128)S(1)} %stack.35.place, ...), custom_call_target="tpu_custom_call" | custom-call | tf_op jit(solution)/shard_map/pallas_call | solution.py:860
  34.9 16.7 %all_to_all.11.received = f32[8,15,8,128]{3,2,1,0:T(8,128)S(1)} all-to-all(f32[8,15,8,128]{3,2,1,0:T(8,128)S(1)} %get-tuple-element.40), channel_id=1, replica_groups=mesh['gx'=8,'gy'=4] {'gx'}, dimensions={0} | all-to-all | bytes 983040 | tf_op jit(solution)/shard_map/all_to_all | solution.py:873
  51.7 4.1 %shard_map.80 = (f32[8,16,16,128]{3,2,1,0:T(8,128)}, f32[16,16,128]{2,1,0:T(8,128)}) custom-call(s32[9]{0:T(128)S(1)} %stack.35.place, f32[8,15,8,128]{3,2,1,0:T(8,128)S(1)} %all_to_all.11.received, f32[16,16,8,128]{3,2,1,0:T(8,128)S(1)} %get-tuple-element.35.first, f32[48,16,128]{2,1,0:T(8,128)S(1)} %get-tuple-element.32.costs, ...), custom_call_target="tpu_custom_call" | custom-call | tf_op jit(solution)/shard_map/pallas_call | solution.py:860
Async XLA Ops:
  3.6 6.9 %collective-permute-start = (f32[104,128]{1,0:T(8,128)S(1)}, f32[104,128]{1,0:T(8,128)S(1)}, u32[]{:S(2)}, u32[]{:S(2)}) collective-permute-start(f32[104,128]{1,0:T(8,128)S(1)} %get-tuple-element.30), channel_id=1, source_target_pairs={{0,1},{1,2},{2,3},{3,0},{4,5},{5,6},{6,7},{7,4},{8,9},{9,10},{10,1... | collective-permute-start | bytes 159752 | tf_op jit(solution)/shard_map/ppermute | solution.py:878
  4.1 6.4 %collective-permute-start.1 = (f32[104,128]{1,0:T(8,128)S(1)}, f32[104,128]{1,0:T(8,128)S(1)}, u32[]{:S(2)}, u32[]{:S(2)}) collective-permute-start(f32[104,128]{1,0:T(8,128)S(1)} %get-tuple-element.31), channel_id=1, source_target_pairs={{0,3},{1,0},{2,1},{3,2},{4,7},{5,4},{6,5},{7,6},{8,11},{9,8},{10,9... | collective-permute-start | bytes 159752 | tf_op jit(solution)/shard_map/ppermute | solution.py:878
  6.1 4.4 %collective-permute-start.2 = (f32[8,128]{1,0:T(8,128)S(1)}, f32[8,128]{1,0:T(8,128)S(1)}, u32[]{:S(2)}, u32[]{:S(2)}) collective-permute-start(f32[8,128]{1,0:T(8,128)S(1)} %get-tuple-element.29.mine), channel_id=1, source_target_pairs={{0,2},{1,3},{2,0},{3,1},{4,6},{5,7},{6,4},{7,5},{8,10},{9,11},{10,... | collective-permute-start | bytes 12296 | tf_op jit(solution)/shard_map/ppermute | solution.py:878

commit v3 on v2

--- a/solution.py
+++ b/solution.py
@@ -13,8 +13,7 @@
 LOG2E = math.log2(math.e)
 RATE = LOG2E / TAU
 BIG = 10000.0 * RATE
-UNROLL = 8
-CHUNKS = 4
+CHUNKS = 2
 VMEM = pl.BlockSpec(memory_space=pltpu.VMEM)
 FAR = pl.BlockSpec(memory_space=pl.ANY)
 SMEM = pl.BlockSpec(memory_space=pltpu.SMEM)
@@ -69,15 +68,6 @@
     for i in range(count):
         carry = step(i, carry)
     return carry
-
-
-def by_steps(count, step, carry):
-    def group(i, carry):
-        for j in range(UNROLL):
-            carry = step(i * UNROLL + j, carry)
-        return carry
-
-    return lax.fori_loop(0, count // UNROLL, group, carry)
 
 
 def packed(left, right):

time: 56 us -> 55.7 us (level)
  no operation moved by 1% of the time
where the time goes in v3:
time: 55.7 us; the launch traced here: 55.5 us
  blocking collectives  35 us (63%)
  Pallas kernels  12.9 us (23%)
  starting transfers between devices  4.74 us (9%)
  waiting for transfers between devices  2.16 us (4%)
  between operations  0.66 us (1%)
    all_to_all x2, blocking collectives, traded(): return lax.all_to_all(message, 'gx', 0, 0, tiled=True)  35 us
    pallas_call x4, Pallas kernels, call(): pl.pallas_call(kernel, out_shape=out, in_specs=[SMEM] * scalars + [FAR] *...  12.9 us
    ppermute x3, starting transfers between devices, rotated(): lax.ppermute(value, axis, [(i, (i + by) % count) for i in range(count)])  4.74 us
    ppermute x3, waiting for transfers between devices, rotated(): lax.ppermute(value, axis, [(i, (i + by) % count) for i in range(count)])  2.16 us
  transfers between devices with their start and end apart: 3, of which 1 were waited for; matrix products, arithmetic and copies ran while one was open for 0% of the time, Pallas kernels for 0%

profile of v3, /device:TPU:0, one launch (start us, length us, event | category | flops | bytes accessed | tf_op | source)
XLA Modules:
  0.0 55.5 jit_solution(11806076374837763813)
XLA Ops:
  0.6 0.1 stack.35.place
  0.7 2.6 %shard_map.77 = (f32[16,16,8,128]{3,2,1,0:T(8,128)S(1)}, f32[48,16,128]{2,1,0:T(8,128)S(1)}, f32[6,16,128]{2,1,0:T(8,128)S(1)}, f32[176,128]{1,0:T(8,128)S(1)}, ...) custom-call(s32[9]{0:T(128)S(1)} %stack.35.place, s32[8]{0:T(128)} %source_far.1, ...), custom_call_target="tpu_custom_call" | custom-call | tf_op jit(solution)/shard_map/pallas_call | solution.py:850
  3.3 0.5 collective-permute-start
  3.8 2.0 %collective-permute-start.1 = (f32[104,128]{1,0:T(8,128)S(1)}, f32[104,128]{1,0:T(8,128)S(1)}, u32[]{:S(2)}, u32[]{:S(2)}) collective-permute-start(f32[104,128]{1,0:T(8,128)S(1)} %get-tuple-element.31), channel_id=1, source_target_pairs={{0,3},{1,0},{2,1},{3,2},{4,7},{5,4},{6,5},{7,6},{8,11},{9,8},{10,9... | collective-permute-start | bytes 159752 | tf_op jit(solution)/shard_map/ppermute | solution.py:868
  5.8 2.2 %collective-permute-start.2 = (f32[8,128]{1,0:T(8,128)S(1)}, f32[8,128]{1,0:T(8,128)S(1)}, u32[]{:S(2)}, u32[]{:S(2)}) collective-permute-start(f32[8,128]{1,0:T(8,128)S(1)} %get-tuple-element.29.mine), channel_id=1, source_target_pairs={{0,2},{1,3},{2,0},{3,1},{4,6},{5,7},{6,4},{7,5},{8,10},{9,11},{10,... | collective-permute-start | bytes 12296 | tf_op jit(solution)/shard_map/ppermute | solution.py:868
  8.0 2.2 %collective-permute-done.2.rest_0_ = f32[8,128]{1,0:T(8,128)S(1)} collective-permute-done((f32[8,128]{1,0:T(8,128)S(1)}, f32[8,128]{1,0:T(8,128)S(1)}, u32[]{:S(2)}, u32[]{:S(2)}) %collective-permute-start.2) | collective-permute-done | bytes 4128 | tf_op jit(solution)/shard_map/ppermute | solution.py:868
  10.2 0.0 collective-permute-done.from_left
  10.2 0.0 collective-permute-done.1.from_right
  10.2 4.2 %shard_map.78 = (f32[16,16,8,128]{3,2,1,0:T(8,128)S(1)}, f32[16,2,8,128]{3,2,1,0:T(8,128)S(1)}, f32[6,16,8,128]{3,2,1,0:T(8,128)S(1)}, f32[16,2,8,128]{3,2,1,0:T...) custom-call(s32[9]{0:T(128)S(1)} %stack.35.place, ...), custom_call_target="tpu_custom_call" | custom-call | tf_op jit(solution)/shard_map/pallas_call | solution.py:850
  14.3 18.2 %all_to_all.10.received = f32[8,13,8,128]{3,2,1,0:T(8,128)S(1)} all-to-all(f32[8,13,8,128]{3,2,1,0:T(8,128)S(1)} %get-tuple-element.34), channel_id=1, replica_groups=mesh['gx'=8,'gy'=4] {'gx'}, dimensions={0} | all-to-all | bytes 851968 | tf_op jit(solution)/shard_map/all_to_all | solution.py:863
  32.6 2.1 %shard_map.79 = (f32[16,8,128]{2,1,0:T(8,128)S(1)}, f32[4,16,8,128]{3,2,1,0:T(8,128)S(1)}, f32[16,8,128]{2,1,0:T(8,128)S(1)}, f32[16,8,128]{2,1,0:T(8,128)S(1)},...) custom-call(s32[9]{0:T(128)S(1)} %stack.35.place, ...), custom_call_target="tpu_custom_call" | custom-call | tf_op jit(solution)/shard_map/pallas_call | solution.py:850
  34.6 16.7 %all_to_all.11.received = f32[8,15,8,128]{3,2,1,0:T(8,128)S(1)} all-to-all(f32[8,15,8,128]{3,2,1,0:T(8,128)S(1)} %get-tuple-element.40), channel_id=1, replica_groups=mesh['gx'=8,'gy'=4] {'gx'}, dimensions={0} | all-to-all | bytes 983040 | tf_op jit(solution)/shard_map/all_to_all | solution.py:863
  51.4 4.1 %shard_map.80 = (f32[8,16,16,128]{3,2,1,0:T(8,128)}, f32[16,16,128]{2,1,0:T(8,128)}) custom-call(s32[9]{0:T(128)S(1)} %stack.35.place, f32[8,15,8,128]{3,2,1,0:T(8,128)S(1)} %all_to_all.11.received, f32[16,16,8,128]{3,2,1,0:T(8,128)S(1)} %get-tuple-element.35.first, f32[48,16,128]{2,1,0:T(8,128)S(1)} %get-tuple-element.32.costs, ...), custom_call_target="tpu_custom_call" | custom-call | tf_op jit(solution)/shard_map/pallas_call | solution.py:850
Async XLA Ops:
  3.3 6.9 %collective-permute-start = (f32[104,128]{1,0:T(8,128)S(1)}, f32[104,128]{1,0:T(8,128)S(1)}, u32[]{:S(2)}, u32[]{:S(2)}) collective-permute-start(f32[104,128]{1,0:T(8,128)S(1)} %get-tuple-element.30), channel_id=1, source_target_pairs={{0,1},{1,2},{2,3},{3,0},{4,5},{5,6},{6,7},{7,4},{8,9},{9,10},{10,1... | collective-permute-start | bytes 159752 | tf_op jit(solution)/shard_map/ppermute | solution.py:868
  3.8 6.4 %collective-permute-start.1 = (f32[104,128]{1,0:T(8,128)S(1)}, f32[104,128]{1,0:T(8,128)S(1)}, u32[]{:S(2)}, u32[]{:S(2)}) collective-permute-start(f32[104,128]{1,0:T(8,128)S(1)} %get-tuple-element.31), channel_id=1, source_target_pairs={{0,3},{1,0},{2,1},{3,2},{4,7},{5,4},{6,5},{7,6},{8,11},{9,8},{10,9... | collective-permute-start | bytes 159752 | tf_op jit(solution)/shard_map/ppermute | solution.py:868
  5.8 4.4 %collective-permute-start.2 = (f32[8,128]{1,0:T(8,128)S(1)}, f32[8,128]{1,0:T(8,128)S(1)}, u32[]{:S(2)}, u32[]{:S(2)}) collective-permute-start(f32[8,128]{1,0:T(8,128)S(1)} %get-tuple-element.29.mine), channel_id=1, source_target_pairs={{0,2},{1,3},{2,0},{3,1},{4,6},{5,7},{6,4},{7,5},{8,10},{9,11},{10,... | collective-permute-start | bytes 12296 | tf_op jit(solution)/shard_map/ppermute | solution.py:868
